TPU v7x, 32 devices: a whole 2x2x4 slice. The times are simulated.
32 devices in a mesh: section: 4 (over z), row: 4 (over x, core), col: 2 (over y).
Axes of the slice: x: 2, y: 2, z: 4, core: 2. Of those that a mesh axis runs over, the one named last changes fastest.
Arguments:
- state: bfloat16 [4, 128, 64, 256], P('section', 'row', 'col'), may hold values from -6 to 6
- fresh: bfloat16 [128, 64, 256], P('row', 'col'), may hold values from -6 to 6
- conv_first: bfloat16 [4, 3, 3, 256, 256], P('section'), may hold values from -0.125 to 0.125
- conv_second: bfloat16 [4, 3, 3, 256, 256], P('section'), may hold values from -0.125 to 0.125
- gains: float32 [4, 2, 256], P('section'), may hold values from 0.1 to 1.9
- shifts: float32 [4, 2, 256], P('section'), may hold values from -2.4 to 2.4
Outputs:
- blocks: bfloat16 [2, 4, 128, 64, 256], P(None, 'section', 'row', 'col')
All inputs are finite; a program needn't handle non-finite values.
Results may differ from a plain program's by a relative error of at most 0.005.
Values may be sent and summed in bfloat16 or wider, within the bound.
A program may use at most 64 MiB of HBM per device.

v0:
```python
import jax
import jax.numpy as jnp
from jax import lax
from jax.sharding import PartitionSpec as P

TICKS = 2


def extended(block, sides, width):
    for axis, dim in sides:
        count = lax.axis_size(axis)
        forward = [(i, i + 1) for i in range(count - 1)]
        backward = [(target, source) for source, target in forward]
        low = lax.ppermute(
            lax.slice_in_dim(block, block.shape[dim] - width, None, axis=dim), axis, forward
        )
        high = lax.ppermute(lax.slice_in_dim(block, 0, width, axis=dim), axis, backward)
        block = jnp.concatenate([low, block, high], axis=dim)
    return block


def shifted(x, axis, by):
    devices = lax.axis_size(axis)
    pairs = [(i, i + by) for i in range(devices) if 0 <= i + by < devices]
    return lax.ppermute(x, axis, pairs)


def convolve(padded, kernel):
    out_rows = padded.shape[0] - 2
    out_cols = padded.shape[1] - 2
    channels = padded.shape[2]
    stacked = jnp.concatenate(
        [padded[:, col_tap : col_tap + out_cols] for col_tap in range(3)], axis=2
    )
    summed = jnp.zeros((out_rows * out_cols, kernel.shape[3]), jnp.float32)
    for row_tap in range(3):
        summed = summed + jnp.dot(
            stacked[row_tap : row_tap + out_rows].reshape(out_rows * out_cols, 3 * channels),
            kernel[row_tap].reshape(3 * channels, kernel.shape[3]),
            preferred_element_type=jnp.float32,
        )
    return summed.reshape(out_rows, out_cols, kernel.shape[3])


def section_block(features, first_kernel, second_kernel, gain_pair, shift_pair):
    padded = extended(features, (("row", 0), ("col", 1)), 1)
    hidden = jax.nn.relu(gain_pair[0] * convolve(padded, first_kernel) + shift_pair[0]).astype(
        jnp.bfloat16
    )
    hidden_padded = extended(hidden, (("row", 0), ("col", 1)), 1)
    second_out = convolve(hidden_padded, second_kernel)
    summed = features.astype(jnp.float32) + gain_pair[1] * second_out + shift_pair[1]
    return jax.nn.relu(summed).astype(jnp.bfloat16)


def per_device(state, fresh, conv_first, conv_second, gains, shifts):
    features = state[0]
    results = []
    for tick_index in range(TICKS):
        output = section_block(features, conv_first[0], conv_second[0], gains[0], shifts[0])
        results.append(output)
        if tick_index + 1 < TICKS:
            arrived = shifted(output, "section", 1)
            features = jnp.where(lax.axis_index("section") == 0, fresh, arrived)
    return jnp.stack(results)[:, None]


def solution(mesh):
    in_specs = (
        P("section", "row", "col", None),
        P("row", "col", None),
        P("section", None, None, None, None),
        P("section", None, None, None, None),
        P("section", None, None),
        P("section", None, None),
    )
    out_specs = P(None, "section", "row", "col", None)
    return jax.shard_map(
        per_device, mesh=mesh, in_specs=in_specs, out_specs=out_specs, check_vma=False
    )
```

profile of v0, /device:TPU:17, one launch (start us, length us, event | category | flops | bytes accessed | tf_op | source)
XLA Modules:
  0.0 96.6 jit_solution(9328777166244554102)
XLA Ops:
  0.0 0.8 slice_bitcast_fusion.1
  0.8 3.7 %collective-permute-start = (bf16[1,32,256]{2,1,0:T(8,128)(2,1)S(1)}, bf16[1,32,256]{2,1,0:T(8,128)(2,1)S(1)}, u32[]{:S(2)}, u32[]{:S(2)}) collective-permute-start(bf16[1,32,256]{2,1,0:T(8,128)(2,1)S(1)} %get-tuple-element.37), channel_id=1, source_target_pairs={{0,2},{2,4},{4,6},{1,3},{3,5},{5,7},{8,10},{10,12},{12,14},{9,11},... | collective-permute-start | bytes 49160 | tf_op jit(solution)/shard_map/ppermute | solution.py:14
  4.5 1.9 %collective-permute-start.1 = (bf16[1,32,256]{2,1,0:T(8,128)(2,1)S(1)}, bf16[1,32,256]{2,1,0:T(8,128)(2,1)S(1)}, u32[]{:S(2)}, u32[]{:S(2)}) collective-permute-start(bf16[1,32,256]{2,1,0:T(8,128)(2,1)S(1)} %get-tuple-element.38), channel_id=1, source_target_pairs={{2,0},{4,2},{6,4},{3,1},{5,3},{7,5},{10,8},{12,10},{14,12},{11,9},... | collective-permute-start | bytes 49160 | tf_op jit(solution)/shard_map/ppermute | solution.py:17
  6.4 1.3 %fusion.18 = (bf16[1,1,3,256,256]{4,3,2,1,0:T(8,128)(2,1)S(1)}, bf16[1,1,3,256,256]{4,3,2,1,0:T(8,128)(2,1)S(1)}, bf16[1,1,3,256,256]{4,3,2,1,0:T(8,128)(2,1)S(1)}) fusion(bf16[1,3,3,256,256]{4,3,2,1,0:T(8,128)(2,1)} %param.8), kind=kLoop, calls=%fused_computation.67 | loop fusion | bytes 2359296 | tf_op jit(solution)/shard_map/slice | solution.py:39
  7.8 1.8 %collective-permute-done.1 = bf16[1,32,256]{2,1,0:T(8,128)(2,1)S(1)} collective-permute-done((bf16[1,32,256]{2,1,0:T(8,128)(2,1)S(1)}, bf16[1,32,256]{2,1,0:T(8,128)(2,1)S(1)}, u32[]{:S(2)}, u32[]{:S(2)}) %collective-permute-start.1) | collective-permute-done | bytes 16416 | tf_op jit(solution)/shard_map/ppermute | solution.py:17
  9.6 0.1 pad_maximum_fusion.35
  9.6 3.1 %collective-permute-start.2 = (bf16[34,1,256]{2,1,0:T(2,128)(2,1)S(1)}, bf16[34,1,256]{2,1,0:T(2,128)(2,1)S(1)}, u32[]{:S(2)}, u32[]{:S(2)}) collective-permute-start(bf16[34,1,256]{2,1,0:T(2,128)(2,1)S(1)} %get-tuple-element.29), channel_id=1, source_target_pairs={{0,1},{2,3},{4,5},{6,7},{8,9},{10,11},{12,13},{14,15},{16,17},{18,... | collective-permute-start | bytes 52232 | tf_op jit(solution)/shard_map/ppermute | solution.py:14
  12.8 1.3 %collective-permute-start.3 = (bf16[34,1,256]{2,1,0:T(2,128)(2,1)S(1)}, bf16[34,1,256]{2,1,0:T(2,128)(2,1)S(1)}, u32[]{:S(2)}, u32[]{:S(2)}) collective-permute-start(bf16[34,1,256]{2,1,0:T(2,128)(2,1)S(1)} %get-tuple-element.30), channel_id=1, source_target_pairs={{1,0},{3,2},{5,4},{7,6},{9,8},{11,10},{13,12},{15,14},{17,16},{19,... | collective-permute-start | bytes 52232 | tf_op jit(solution)/shard_map/ppermute | solution.py:17
  14.1 0.0 collective-permute-done.2
  14.1 3.3 %collective-permute-done.3 = bf16[34,1,256]{2,1,0:T(2,128)(2,1)S(1)} collective-permute-done((bf16[34,1,256]{2,1,0:T(2,128)(2,1)S(1)}, bf16[34,1,256]{2,1,0:T(2,128)(2,1)S(1)}, u32[]{:S(2)}, u32[]{:S(2)}) %collective-permute-start.3) | collective-permute-done | bytes 17440 | tf_op jit(solution)/shard_map/ppermute | solution.py:17
  17.4 1.9 %fusion.6 = bf16[34,32,768]{2,1,0:T(8,128)(2,1)S(1)} fusion(bf16[34,1,256]{2,1,0:T(2,128)(2,1)S(1)} %collective-permute-done.3, bf16[1,32,256]{2,1,0:T(8,128)(2,1)S(1)} %collective-permute-done.1, bf16[32,32,256]{2,1,0:T(8,128)(2,1)S(1)} %bitcast.64, bf16[1,32,256]{2,1,0:T(8,128)(2,1)S(1)} %collective-permute-done, ...), kind=kLoop, calls=%fused_computation.25 | loop fusion | flops 18382848 | bytes 2263040 | tf_op jit(solution)/shard_map/concatenate | solution.py:32
  19.3 0.6 fusion.16
  19.9 0.6 fusion.25
  20.5 0.6 fusion.24
  21.1 0.6 fusion.11
  21.7 0.0 copy-start.3
  21.7 0.1 maximum_convert_fusion.4
  21.9 3.5 %collective-permute-start.4 = (bf16[1,32,256]{2,1,0:T(8,128)(2,1)S(1)}, bf16[1,32,256]{2,1,0:T(8,128)(2,1)S(1)}, u32[]{:S(2)}, u32[]{:S(2)}) collective-permute-start(bf16[1,32,256]{2,1,0:T(8,128)(2,1)S(1)} %get-tuple-element.35), channel_id=1, source_target_pairs={{0,2},{2,4},{4,6},{1,3},{3,5},{5,7},{8,10},{10,12},{12,14},{9,11},... | collective-permute-start | bytes 49160 | tf_op jit(solution)/shard_map/ppermute | solution.py:14
  25.4 1.9 %collective-permute-start.5 = (bf16[1,32,256]{2,1,0:T(8,128)(2,1)S(1)}, bf16[1,32,256]{2,1,0:T(8,128)(2,1)S(1)}, u32[]{:S(2)}, u32[]{:S(2)}) collective-permute-start(bf16[1,32,256]{2,1,0:T(8,128)(2,1)S(1)} %get-tuple-element.36), channel_id=1, source_target_pairs={{2,0},{4,2},{6,4},{3,1},{5,3},{7,5},{10,8},{12,10},{14,12},{11,9},... | collective-permute-start | bytes 49160 | tf_op jit(solution)/shard_map/ppermute | solution.py:17
  27.3 0.0 collective-permute-done.4
  27.3 3.1 %collective-permute-done.5 = bf16[1,32,256]{2,1,0:T(8,128)(2,1)S(1)} collective-permute-done((bf16[1,32,256]{2,1,0:T(8,128)(2,1)S(1)}, bf16[1,32,256]{2,1,0:T(8,128)(2,1)S(1)}, u32[]{:S(2)}, u32[]{:S(2)}) %collective-permute-start.5) | collective-permute-done | bytes 16416 | tf_op jit(solution)/shard_map/ppermute | solution.py:17
  30.4 0.1 pad_maximum_fusion.32
  30.5 1.3 %collective-permute-start.6 = (bf16[34,1,256]{2,1,0:T(2,128)(2,1)S(1)}, bf16[34,1,256]{2,1,0:T(2,128)(2,1)S(1)}, u32[]{:S(2)}, u32[]{:S(2)}) collective-permute-start(bf16[34,1,256]{2,1,0:T(2,128)(2,1)S(1)} %get-tuple-element.27), channel_id=1, source_target_pairs={{0,1},{2,3},{4,5},{6,7},{8,9},{10,11},{12,13},{14,15},{16,17},{18,... | collective-permute-start | bytes 52232 | tf_op jit(solution)/shard_map/ppermute | solution.py:14
  31.8 1.3 %collective-permute-start.7 = (bf16[34,1,256]{2,1,0:T(2,128)(2,1)S(1)}, bf16[34,1,256]{2,1,0:T(2,128)(2,1)S(1)}, u32[]{:S(2)}, u32[]{:S(2)}) collective-permute-start(bf16[34,1,256]{2,1,0:T(2,128)(2,1)S(1)} %get-tuple-element.28), channel_id=1, source_target_pairs={{1,0},{3,2},{5,4},{7,6},{9,8},{11,10},{13,12},{15,14},{17,16},{19,... | collective-permute-start | bytes 52232 | tf_op jit(solution)/shard_map/ppermute | solution.py:17
  33.1 0.1 fusion.17
  33.2 3.3 %collective-permute-done.7 = bf16[34,1,256]{2,1,0:T(2,128)(2,1)S(1)} collective-permute-done((bf16[34,1,256]{2,1,0:T(2,128)(2,1)S(1)}, bf16[34,1,256]{2,1,0:T(2,128)(2,1)S(1)}, u32[]{:S(2)}, u32[]{:S(2)}) %collective-permute-start.7) | collective-permute-done | bytes 17440 | tf_op jit(solution)/shard_map/ppermute | solution.py:17
  36.5 1.9 %fusion.4 = bf16[34,32,768]{2,1,0:T(8,128)(2,1)S(1)} fusion(bf16[34,1,256]{2,1,0:T(2,128)(2,1)S(1)} %collective-permute-done.7, bf16[1,32,256]{2,1,0:T(8,128)(2,1)S(1)} %collective-permute-done.5, bf16[32,32,256]{2,1,0:T(8,128)(2,1)S(1)} %maximum_convert_fusion.4, bf16[1,32,256]{2,1,0:T(8,128)(2,1)S(1)} %collective-permute-done.4, ...), kind=kLoop, calls=%fused_computation.17 | loop fusion | flops 18382848 | bytes 2263040 | tf_op jit(solution)/shard_map/concatenate | solution.py:32
  38.4 0.6 fusion.15
  39.0 0.6 fusion.27
  39.6 0.6 fusion.26
  40.2 0.6 fusion.10
  40.8 1.0 %maximum_convert_fusion.2 = bf16[32,32,256]{2,1,0:T(8,128)(2,1)} fusion(f32[32,32,256]{2,1,0:T(8,128)S(1)} %bitcast.61, f32[256]{0:T(256)S(1)} %bitcast.95, f32[256]{0:T(256)S(1)} %bitcast.92, bf16[1,32,32,256]{3,2,1,0:T(8,128)(2,1)S(1)} %copy-done), kind=kLoop, calls=%fused_computation.43 | loop fusion | flops 1572864 | bytes 2099200 | tf_op jit(solution)/shard_map/convert_element_type | solution.py:53
  41.8 3.2 %collective-permute-start.8 = (bf16[32,32,256]{2,1,0:T(8,128)(2,1)}, bf16[32,32,256]{2,1,0:T(8,128)(2,1)}, u32[]{:S(2)}, u32[]{:S(2)}) collective-permute-start(bf16[32,32,256]{2,1,0:T(8,128)(2,1)} %maximum_convert_fusion.2), channel_id=1, source_target_pairs={{0,8},{8,16},{16,24},{1,9},{9,17},{17,25},{2,10},{10,18},{18,26},{... | collective-permute-start | bytes 1572872 | tf_op jit(solution)/shard_map/ppermute | solution.py:25
  45.0 12.8 %collective-permute-done.8 = bf16[32,32,256]{2,1,0:T(8,128)(2,1)} collective-permute-done((bf16[32,32,256]{2,1,0:T(8,128)(2,1)}, bf16[32,32,256]{2,1,0:T(8,128)(2,1)}, u32[]{:S(2)}, u32[]{:S(2)}) %collective-permute-start.8) | collective-permute-done | bytes 524320 | tf_op jit(solution)/shard_map/ppermute | solution.py:25
  57.8 1.1 %broadcast_select_fusion = bf16[32,32,256]{2,1,0:T(8,128)(2,1)S(1)} fusion(bf16[32,32,256]{2,1,0:T(8,128)(2,1)} %param.7, bf16[32,32,256]{2,1,0:T(8,128)(2,1)} %collective-permute-done.8, pred[]{:T(512)S(6)} %eq.3), kind=kLoop, calls=%fused_computation.47 | loop fusion | flops 262144 | bytes 1572865 | tf_op jit(solution)/shard_map/jit(_where)/select_n | solution.py:64
  58.9 1.9 %collective-permute-start.9 = (bf16[1,32,256]{2,1,0:T(8,128)(2,1)S(1)}, bf16[1,32,256]{2,1,0:T(8,128)(2,1)S(1)}, u32[]{:S(2)}, u32[]{:S(2)}) collective-permute-start(bf16[1,32,256]{2,1,0:T(8,128)(2,1)S(1)} %get-tuple-element.33), channel_id=1, source_target_pairs={{0,2},{2,4},{4,6},{1,3},{3,5},{5,7},{8,10},{10,12},{12,14},{9,11},... | collective-permute-start | bytes 49160 | tf_op jit(solution)/shard_map/ppermute | solution.py:14
  60.8 2.4 %collective-permute-start.10 = (bf16[1,32,256]{2,1,0:T(8,128)(2,1)S(1)}, bf16[1,32,256]{2,1,0:T(8,128)(2,1)S(1)}, u32[]{:S(2)}, u32[]{:S(2)}) collective-permute-start(bf16[1,32,256]{2,1,0:T(8,128)(2,1)S(1)} %get-tuple-element.34), channel_id=1, source_target_pairs={{2,0},{4,2},{6,4},{3,1},{5,3},{7,5},{10,8},{12,10},{14,12},{11,9},... | collective-permute-start | bytes 49160 | tf_op jit(solution)/shard_map/ppermute | solution.py:17
  63.2 2.6 %collective-permute-done.10 = bf16[1,32,256]{2,1,0:T(8,128)(2,1)S(1)} collective-permute-done((bf16[1,32,256]{2,1,0:T(8,128)(2,1)S(1)}, bf16[1,32,256]{2,1,0:T(8,128)(2,1)S(1)}, u32[]{:S(2)}, u32[]{:S(2)}) %collective-permute-start.10) | collective-permute-done | bytes 16416 | tf_op jit(solution)/shard_map/ppermute | solution.py:17
  65.9 0.1 pad_maximum_fusion.29
  65.9 1.3 %collective-permute-start.11 = (bf16[34,1,256]{2,1,0:T(2,128)(2,1)S(1)}, bf16[34,1,256]{2,1,0:T(2,128)(2,1)S(1)}, u32[]{:S(2)}, u32[]{:S(2)}) collective-permute-start(bf16[34,1,256]{2,1,0:T(2,128)(2,1)S(1)} %get-tuple-element.25), channel_id=1, source_target_pairs={{0,1},{2,3},{4,5},{6,7},{8,9},{10,11},{12,13},{14,15},{16,17},{18,... | collective-permute-start | bytes 52232 | tf_op jit(solution)/shard_map/ppermute | solution.py:14
  67.2 1.3 %collective-permute-start.12 = (bf16[34,1,256]{2,1,0:T(2,128)(2,1)S(1)}, bf16[34,1,256]{2,1,0:T(2,128)(2,1)S(1)}, u32[]{:S(2)}, u32[]{:S(2)}) collective-permute-start(bf16[34,1,256]{2,1,0:T(2,128)(2,1)S(1)} %get-tuple-element.26), channel_id=1, source_target_pairs={{1,0},{3,2},{5,4},{7,6},{9,8},{11,10},{13,12},{15,14},{17,16},{19,... | collective-permute-start | bytes 52232 | tf_op jit(solution)/shard_map/ppermute | solution.py:17
  68.5 3.4 %collective-permute-done.12 = bf16[34,1,256]{2,1,0:T(2,128)(2,1)S(1)} collective-permute-done((bf16[34,1,256]{2,1,0:T(2,128)(2,1)S(1)}, bf16[34,1,256]{2,1,0:T(2,128)(2,1)S(1)}, u32[]{:S(2)}, u32[]{:S(2)}) %collective-permute-start.12) | collective-permute-done | bytes 17440 | tf_op jit(solution)/shard_map/ppermute | solution.py:17
  71.9 1.9 %fusion.2 = bf16[34,32,768]{2,1,0:T(8,128)(2,1)S(1)} fusion(bf16[34,1,256]{2,1,0:T(2,128)(2,1)S(1)} %collective-permute-done.12, bf16[1,32,256]{2,1,0:T(8,128)(2,1)S(1)} %collective-permute-done.10, bf16[32,32,256]{2,1,0:T(8,128)(2,1)S(1)} %broadcast_select_fusion, bf16[1,32,256]{2,1,0:T(8,128)(2,1)S(1)} %collective-permute-done.9, ...), kind=kLoop, calls=%fused_computation.9 | loop fusion | flops 18382848 | bytes 2263040 | tf_op jit(solution)/shard_map/concatenate | solution.py:32
  73.8 0.6 fusion.14
  74.4 0.6 fusion.29
  75.0 0.6 fusion.28
  75.5 0.6 fusion.9
  76.1 0.1 maximum_convert_fusion.1
  76.3 3.2 %collective-permute-start.13 = (bf16[1,32,256]{2,1,0:T(8,128)(2,1)S(1)}, bf16[1,32,256]{2,1,0:T(8,128)(2,1)S(1)}, u32[]{:S(2)}, u32[]{:S(2)}) collective-permute-start(bf16[1,32,256]{2,1,0:T(8,128)(2,1)S(1)} %get-tuple-element.31), channel_id=1, source_target_pairs={{0,2},{2,4},{4,6},{1,3},{3,5},{5,7},{8,10},{10,12},{12,14},{9,11},... | collective-permute-start | bytes 49160 | tf_op jit(solution)/shard_map/ppermute | solution.py:14
  79.5 1.9 %collective-permute-start.14 = (bf16[1,32,256]{2,1,0:T(8,128)(2,1)S(1)}, bf16[1,32,256]{2,1,0:T(8,128)(2,1)S(1)}, u32[]{:S(2)}, u32[]{:S(2)}) collective-permute-start(bf16[1,32,256]{2,1,0:T(8,128)(2,1)S(1)} %get-tuple-element.32), channel_id=1, source_target_pairs={{2,0},{4,2},{6,4},{3,1},{5,3},{7,5},{10,8},{12,10},{14,12},{11,9},... | collective-permute-start | bytes 49160 | tf_op jit(solution)/shard_map/ppermute | solution.py:17
  81.5 3.1 %collective-permute-done.14 = bf16[1,32,256]{2,1,0:T(8,128)(2,1)S(1)} collective-permute-done((bf16[1,32,256]{2,1,0:T(8,128)(2,1)S(1)}, bf16[1,32,256]{2,1,0:T(8,128)(2,1)S(1)}, u32[]{:S(2)}, u32[]{:S(2)}) %collective-permute-start.14) | collective-permute-done | bytes 16416 | tf_op jit(solution)/shard_map/ppermute | solution.py:17
  84.6 0.1 pad_maximum_fusion.26
  84.6 1.3 %collective-permute-start.15 = (bf16[34,1,256]{2,1,0:T(2,128)(2,1)S(1)}, bf16[34,1,256]{2,1,0:T(2,128)(2,1)S(1)}, u32[]{:S(2)}, u32[]{:S(2)}) collective-permute-start(bf16[34,1,256]{2,1,0:T(2,128)(2,1)S(1)} %get-tuple-element.23), channel_id=1, source_target_pairs={{0,1},{2,3},{4,5},{6,7},{8,9},{10,11},{12,13},{14,15},{16,17},{18,... | collective-permute-start | bytes 52232 | tf_op jit(solution)/shard_map/ppermute | solution.py:14
  86.0 1.5 %collective-permute-start.16 = (bf16[34,1,256]{2,1,0:T(2,128)(2,1)S(1)}, bf16[34,1,256]{2,1,0:T(2,128)(2,1)S(1)}, u32[]{:S(2)}, u32[]{:S(2)}) collective-permute-start(bf16[34,1,256]{2,1,0:T(2,128)(2,1)S(1)} %get-tuple-element.24), channel_id=1, source_target_pairs={{1,0},{3,2},{5,4},{7,6},{9,8},{11,10},{13,12},{15,14},{17,16},{19,... | collective-permute-start | bytes 52232 | tf_op jit(solution)/shard_map/ppermute | solution.py:17
  87.5 0.2 maximum_convert_fusion.3
  87.7 3.0 %collective-permute-done.16 = bf16[34,1,256]{2,1,0:T(2,128)(2,1)S(1)} collective-permute-done((bf16[34,1,256]{2,1,0:T(2,128)(2,1)S(1)}, bf16[34,1,256]{2,1,0:T(2,128)(2,1)S(1)}, u32[]{:S(2)}, u32[]{:S(2)}) %collective-permute-start.16) | collective-permute-done | bytes 17440 | tf_op jit(solution)/shard_map/ppermute | solution.py:17
  90.7 1.9 %fusion = bf16[34,32,768]{2,1,0:T(8,128)(2,1)S(1)} fusion(bf16[34,1,256]{2,1,0:T(2,128)(2,1)S(1)} %collective-permute-done.16, bf16[1,32,256]{2,1,0:T(8,128)(2,1)S(1)} %collective-permute-done.14, bf16[32,32,256]{2,1,0:T(8,128)(2,1)S(1)} %maximum_convert_fusion.1, bf16[1,32,256]{2,1,0:T(8,128)(2,1)S(1)} %collective-permute-done.13, ...), kind=kLoop, calls=%fused_computation.1 | loop fusion | flops 18382848 | bytes 2263040 | tf_op jit(solution)/shard_map/concatenate | solution.py:32
  92.5 0.6 fusion.13
  93.1 0.4 copy-done.2
  93.5 0.6 fusion.31
  94.1 0.6 fusion.30
  94.7 0.6 fusion.8
  95.3 0.2 fusion.12
  95.5 1.1 %maximum_bitcast_fusion = bf16[2,1,32,32,256]{4,3,2,1,0:T(8,128)(2,1)} fusion(bf16[1,32,32,256]{3,2,1,0:T(8,128)(2,1)S(1)} %fusion.12, bf16[1,32,32,256]{3,2,1,0:T(8,128)(2,1)S(1)} %maximum_convert_fusion.3), kind=kLoop, calls=%fused_computation.40 | loop fusion | flops 524288 | bytes 2097152 | tf_op jit(solution)/shard_map/broadcast_in_dim | solution.py:65
  (21 shorter events, 0.1 us)
Async XLA Ops:
  0.0 9.5 %copy-start = (bf16[1,32,32,256]{3,2,1,0:T(8,128)(2,1)S(1)}, bf16[1,32,32,256]{3,2,1,0:T(8,128)(2,1)}, u32[]{:S(2)}) copy-start(bf16[1,32,32,256]{3,2,1,0:T(8,128)(2,1)} %param.6) | copy-start | bytes 1572868
  0.0 7.7 %copy-start.4 = (f32[1,2,256]{2,1,0:T(2,128)S(1)}, f32[1,2,256]{2,1,0:T(2,128)}, u32[]{:S(2)}) copy-start(f32[1,2,256]{2,1,0:T(2,128)} %param.10) | copy-start | bytes 6148
  0.0 14.1 %copy-start.5 = (f32[1,2,256]{2,1,0:T(2,128)S(1)}, f32[1,2,256]{2,1,0:T(2,128)}, u32[]{:S(2)}) copy-start(f32[1,2,256]{2,1,0:T(2,128)} %param.11) | copy-start | bytes 6148
  0.8 6.9 %collective-permute-start = (bf16[1,32,256]{2,1,0:T(8,128)(2,1)S(1)}, bf16[1,32,256]{2,1,0:T(8,128)(2,1)S(1)}, u32[]{:S(2)}, u32[]{:S(2)}) collective-permute-start(bf16[1,32,256]{2,1,0:T(8,128)(2,1)S(1)} %get-tuple-element.37), channel_id=1, source_target_pairs={{0,2},{2,4},{4,6},{1,3},{3,5},{5,7},{8,10},{10,12},{12,14},{9,11},... | collective-permute-start | bytes 49160 | tf_op jit(solution)/shard_map/ppermute | solution.py:14
  4.5 5.1 %collective-permute-start.1 = (bf16[1,32,256]{2,1,0:T(8,128)(2,1)S(1)}, bf16[1,32,256]{2,1,0:T(8,128)(2,1)S(1)}, u32[]{:S(2)}, u32[]{:S(2)}) collective-permute-start(bf16[1,32,256]{2,1,0:T(8,128)(2,1)S(1)} %get-tuple-element.38), channel_id=1, source_target_pairs={{2,0},{4,2},{6,4},{3,1},{5,3},{7,5},{10,8},{12,10},{14,12},{11,9},... | collective-permute-start | bytes 49160 | tf_op jit(solution)/shard_map/ppermute | solution.py:17
  9.6 4.5 %collective-permute-start.2 = (bf16[34,1,256]{2,1,0:T(2,128)(2,1)S(1)}, bf16[34,1,256]{2,1,0:T(2,128)(2,1)S(1)}, u32[]{:S(2)}, u32[]{:S(2)}) collective-permute-start(bf16[34,1,256]{2,1,0:T(2,128)(2,1)S(1)} %get-tuple-element.29), channel_id=1, source_target_pairs={{0,1},{2,3},{4,5},{6,7},{8,9},{10,11},{12,13},{14,15},{16,17},{18,... | collective-permute-start | bytes 52232 | tf_op jit(solution)/shard_map/ppermute | solution.py:14
  12.8 4.7 %collective-permute-start.3 = (bf16[34,1,256]{2,1,0:T(2,128)(2,1)S(1)}, bf16[34,1,256]{2,1,0:T(2,128)(2,1)S(1)}, u32[]{:S(2)}, u32[]{:S(2)}) collective-permute-start(bf16[34,1,256]{2,1,0:T(2,128)(2,1)S(1)} %get-tuple-element.30), channel_id=1, source_target_pairs={{1,0},{3,2},{5,4},{7,6},{9,8},{11,10},{13,12},{15,14},{17,16},{19,... | collective-permute-start | bytes 52232 | tf_op jit(solution)/shard_map/ppermute | solution.py:17
  21.7 11.4 %copy-start.3 = (bf16[1,3,3,256,256]{4,3,2,1,0:T(8,128)(2,1)S(1)}, bf16[1,3,3,256,256]{4,3,2,1,0:T(8,128)(2,1)}, u32[]{:S(2)}) copy-start(bf16[1,3,3,256,256]{4,3,2,1,0:T(8,128)(2,1)} %param.9) | copy-start | bytes 3538948
  21.9 5.4 %collective-permute-start.4 = (bf16[1,32,256]{2,1,0:T(8,128)(2,1)S(1)}, bf16[1,32,256]{2,1,0:T(8,128)(2,1)S(1)}, u32[]{:S(2)}, u32[]{:S(2)}) collective-permute-start(bf16[1,32,256]{2,1,0:T(8,128)(2,1)S(1)} %get-tuple-element.35), channel_id=1, source_target_pairs={{0,2},{2,4},{4,6},{1,3},{3,5},{5,7},{8,10},{10,12},{12,14},{9,11},... | collective-permute-start | bytes 49160 | tf_op jit(solution)/shard_map/ppermute | solution.py:14
  25.4 5.1 %collective-permute-start.5 = (bf16[1,32,256]{2,1,0:T(8,128)(2,1)S(1)}, bf16[1,32,256]{2,1,0:T(8,128)(2,1)S(1)}, u32[]{:S(2)}, u32[]{:S(2)}) collective-permute-start(bf16[1,32,256]{2,1,0:T(8,128)(2,1)S(1)} %get-tuple-element.36), channel_id=1, source_target_pairs={{2,0},{4,2},{6,4},{3,1},{5,3},{7,5},{10,8},{12,10},{14,12},{11,9},... | collective-permute-start | bytes 49160 | tf_op jit(solution)/shard_map/ppermute | solution.py:17
  30.5 2.7 %collective-permute-start.6 = (bf16[34,1,256]{2,1,0:T(2,128)(2,1)S(1)}, bf16[34,1,256]{2,1,0:T(2,128)(2,1)S(1)}, u32[]{:S(2)}, u32[]{:S(2)}) collective-permute-start(bf16[34,1,256]{2,1,0:T(2,128)(2,1)S(1)} %get-tuple-element.27), channel_id=1, source_target_pairs={{0,1},{2,3},{4,5},{6,7},{8,9},{10,11},{12,13},{14,15},{16,17},{18,... | collective-permute-start | bytes 52232 | tf_op jit(solution)/shard_map/ppermute | solution.py:14
  31.8 4.7 %collective-permute-start.7 = (bf16[34,1,256]{2,1,0:T(2,128)(2,1)S(1)}, bf16[34,1,256]{2,1,0:T(2,128)(2,1)S(1)}, u32[]{:S(2)}, u32[]{:S(2)}) collective-permute-start(bf16[34,1,256]{2,1,0:T(2,128)(2,1)S(1)} %get-tuple-element.28), channel_id=1, source_target_pairs={{1,0},{3,2},{5,4},{7,6},{9,8},{11,10},{13,12},{15,14},{17,16},{19,... | collective-permute-start | bytes 52232 | tf_op jit(solution)/shard_map/ppermute | solution.py:17
  33.2 5.8 %copy-start.1 = (bf16[1,1,3,256,256]{4,3,2,1,0:T(8,128)(2,1)}, bf16[1,1,3,256,256]{4,3,2,1,0:T(8,128)(2,1)S(1)}, u32[]{:S(2)}) copy-start(bf16[1,1,3,256,256]{4,3,2,1,0:T(8,128)(2,1)S(1)} %get-tuple-element.18) | copy-start | bytes 1179652
  41.8 16.0 %collective-permute-start.8 = (bf16[32,32,256]{2,1,0:T(8,128)(2,1)}, bf16[32,32,256]{2,1,0:T(8,128)(2,1)}, u32[]{:S(2)}, u32[]{:S(2)}) collective-permute-start(bf16[32,32,256]{2,1,0:T(8,128)(2,1)} %maximum_convert_fusion.2), channel_id=1, source_target_pairs={{0,8},{8,16},{16,24},{1,9},{9,17},{17,25},{2,10},{10,18},{18,26},{... | collective-permute-start | bytes 1572872 | tf_op jit(solution)/shard_map/ppermute | solution.py:25
  58.9 4.3 %collective-permute-start.9 = (bf16[1,32,256]{2,1,0:T(8,128)(2,1)S(1)}, bf16[1,32,256]{2,1,0:T(8,128)(2,1)S(1)}, u32[]{:S(2)}, u32[]{:S(2)}) collective-permute-start(bf16[1,32,256]{2,1,0:T(8,128)(2,1)S(1)} %get-tuple-element.33), channel_id=1, source_target_pairs={{0,2},{2,4},{4,6},{1,3},{3,5},{5,7},{8,10},{10,12},{12,14},{9,11},... | collective-permute-start | bytes 49160 | tf_op jit(solution)/shard_map/ppermute | solution.py:14
  60.8 5.1 %collective-permute-start.10 = (bf16[1,32,256]{2,1,0:T(8,128)(2,1)S(1)}, bf16[1,32,256]{2,1,0:T(8,128)(2,1)S(1)}, u32[]{:S(2)}, u32[]{:S(2)}) collective-permute-start(bf16[1,32,256]{2,1,0:T(8,128)(2,1)S(1)} %get-tuple-element.34), channel_id=1, source_target_pairs={{2,0},{4,2},{6,4},{3,1},{5,3},{7,5},{10,8},{12,10},{14,12},{11,9},... | collective-permute-start | bytes 49160 | tf_op jit(solution)/shard_map/ppermute | solution.py:17
  65.9 2.6 %collective-permute-start.11 = (bf16[34,1,256]{2,1,0:T(2,128)(2,1)S(1)}, bf16[34,1,256]{2,1,0:T(2,128)(2,1)S(1)}, u32[]{:S(2)}, u32[]{:S(2)}) collective-permute-start(bf16[34,1,256]{2,1,0:T(2,128)(2,1)S(1)} %get-tuple-element.25), channel_id=1, source_target_pairs={{0,1},{2,3},{4,5},{6,7},{8,9},{10,11},{12,13},{14,15},{16,17},{18,... | collective-permute-start | bytes 52232 | tf_op jit(solution)/shard_map/ppermute | solution.py:14
  67.2 4.7 %collective-permute-start.12 = (bf16[34,1,256]{2,1,0:T(2,128)(2,1)S(1)}, bf16[34,1,256]{2,1,0:T(2,128)(2,1)S(1)}, u32[]{:S(2)}, u32[]{:S(2)}) collective-permute-start(bf16[34,1,256]{2,1,0:T(2,128)(2,1)S(1)} %get-tuple-element.26), channel_id=1, source_target_pairs={{1,0},{3,2},{5,4},{7,6},{9,8},{11,10},{13,12},{15,14},{17,16},{19,... | collective-permute-start | bytes 52232 | tf_op jit(solution)/shard_map/ppermute | solution.py:17
  76.3 5.1 %collective-permute-start.13 = (bf16[1,32,256]{2,1,0:T(8,128)(2,1)S(1)}, bf16[1,32,256]{2,1,0:T(8,128)(2,1)S(1)}, u32[]{:S(2)}, u32[]{:S(2)}) collective-permute-start(bf16[1,32,256]{2,1,0:T(8,128)(2,1)S(1)} %get-tuple-element.31), channel_id=1, source_target_pairs={{0,2},{2,4},{4,6},{1,3},{3,5},{5,7},{8,10},{10,12},{12,14},{9,11},... | collective-permute-start | bytes 49160 | tf_op jit(solution)/shard_map/ppermute | solution.py:14
  79.5 5.1 %collective-permute-start.14 = (bf16[1,32,256]{2,1,0:T(8,128)(2,1)S(1)}, bf16[1,32,256]{2,1,0:T(8,128)(2,1)S(1)}, u32[]{:S(2)}, u32[]{:S(2)}) collective-permute-start(bf16[1,32,256]{2,1,0:T(8,128)(2,1)S(1)} %get-tuple-element.32), channel_id=1, source_target_pairs={{2,0},{4,2},{6,4},{3,1},{5,3},{7,5},{10,8},{12,10},{14,12},{11,9},... | collective-permute-start | bytes 49160 | tf_op jit(solution)/shard_map/ppermute | solution.py:17
  84.6 3.0 %collective-permute-start.15 = (bf16[34,1,256]{2,1,0:T(2,128)(2,1)S(1)}, bf16[34,1,256]{2,1,0:T(2,128)(2,1)S(1)}, u32[]{:S(2)}, u32[]{:S(2)}) collective-permute-start(bf16[34,1,256]{2,1,0:T(2,128)(2,1)S(1)} %get-tuple-element.23), channel_id=1, source_target_pairs={{0,1},{2,3},{4,5},{6,7},{8,9},{10,11},{12,13},{14,15},{16,17},{18,... | collective-permute-start | bytes 52232 | tf_op jit(solution)/shard_map/ppermute | solution.py:14
  86.0 4.7 %collective-permute-start.16 = (bf16[34,1,256]{2,1,0:T(2,128)(2,1)S(1)}, bf16[34,1,256]{2,1,0:T(2,128)(2,1)S(1)}, u32[]{:S(2)}, u32[]{:S(2)}) collective-permute-start(bf16[34,1,256]{2,1,0:T(2,128)(2,1)S(1)} %get-tuple-element.24), channel_id=1, source_target_pairs={{1,0},{3,2},{5,4},{7,6},{9,8},{11,10},{13,12},{15,14},{17,16},{19,... | collective-permute-start | bytes 52232 | tf_op jit(solution)/shard_map/ppermute | solution.py:17
  92.5 1.0 %copy-start.2 = (bf16[1,1,3,256,256]{4,3,2,1,0:T(8,128)(2,1)S(1)}, bf16[1,1,3,256,256]{4,3,2,1,0:T(8,128)(2,1)}, u32[]{:S(2)}) copy-start(bf16[1,1,3,256,256]{4,3,2,1,0:T(8,128)(2,1)} %copy-done.1) | copy-start | bytes 1179652
where the time goes:
time: 97.4 us; the launch traced here: 96.6 us
  waiting for transfers between devices  36.4 us (37%)
  starting transfers between devices  36.1 us (37%)
  other arithmetic  11.6 us (12%)
  matrix products  7.04 us (7%)
  local copies, waits for them, and re-layouts  4.97 us (5%)
    ppermute x8, waiting for transfers between devices, extended(): lax.ppermute(lax.slice_in_dim(block, 0, width, axis=dim), axis, backward)  23.6 us
    ppermute x8, starting transfers between devices, extended(): lax.ppermute(lax.slice_in_dim(block, block.shape[dim] - width, None, axis...  19.4 us
    ppermute x8, starting transfers between devices, extended(): lax.ppermute(lax.slice_in_dim(block, 0, width, axis=dim), axis, backward)  13.5 us
    ppermute x1, waiting for transfers between devices, shifted(): return lax.ppermute(x, axis, pairs)  12.8 us
    concatenate x4, other arithmetic, convolve(): jnp.concatenate([padded[:, col_tap:col_tap + out_cols] for col_tap in ran...  7.44 us
    dot_general x12, matrix products, convolve(): jnp.dot(stacked[row_tap:row_tap + out_rows].reshape(out_rows * out_cols,...  7.04 us
    ppermute x1, starting transfers between devices, shifted(): return lax.ppermute(x, axis, pairs)  3.2 us
    slice x4, local copies, waits for them, and re-layouts, convolve(): stacked[row_tap:row_tap + out_rows]  2.33 us
  transfers between devices with their start and end apart: 17, of which 9 were waited for; matrix products, arithmetic and copies ran while one was open for 2% of the time, Pallas kernels for 0%

commit v1 on v0

v1 whole, which is shorter than its diff:
```python
import functools

import jax
import jax.numpy as jnp
from jax import lax
from jax.experimental import pallas as pl
from jax.experimental.pallas import tpu as pltpu
from jax.sharding import PartitionSpec as P

TICKS = 2
CHUNK = 8
DIRECTIONS = ((-1, 0), (1, 0), (0, -1), (0, 1), (-1, -1), (-1, 1), (1, -1), (1, 1))
MESH = pl.DeviceIdType.MESH


def kernel(
    sections, rows_n, cols_n,
    state, fresh, first, second, gains, shifts, out,
    x0, x1, out0, out1, w1, w2, stk_x, stk_h,
    out_row, out_col, halo_row, halo_col, halo_cor,
    in_sem, out_sem, send_sem, recv_sem, sec_send, sec_recv,
):
    height, width, chan = x0.shape
    chunks = height // CHUNK
    sec = lax.axis_index("section")
    row = lax.axis_index("row")
    col = lax.axis_index("col")

    def exists(dr, dc):
        return (row + dr >= 0) & (row + dr < rows_n) & (col + dc >= 0) & (col + dc < cols_n)

    def target(dr, dc):
        return {"row": row + dr, "col": col + dc}

    ins = [
        pltpu.make_async_copy(state, x0, in_sem.at[0]),
        pltpu.make_async_copy(first, w1, in_sem.at[1]),
        pltpu.make_async_copy(second, w2, in_sem.at[2]),
    ]
    fresh_copy = pltpu.make_async_copy(fresh, x1, in_sem.at[3])
    for copy in ins:
        copy.start()

    @pl.when(sec == 0)
    def _():
        fresh_copy.start()

    halo_row[...] = jnp.zeros_like(halo_row)
    halo_col[...] = jnp.zeros_like(halo_col)
    halo_cor[...] = jnp.zeros_like(halo_cor)

    barrier = pltpu.get_barrier_semaphore()
    count = jnp.int32(0)
    for dr, dc in DIRECTIONS:
        there = exists(dr, dc)
        count = count + there.astype(jnp.int32)

        @pl.when(there)
        def _(dr=dr, dc=dc):
            pl.semaphore_signal(barrier, inc=1, device_id=target(dr, dc), device_id_type=MESH)

    for ds in (-1, 1):
        there = (sec + ds >= 0) & (sec + ds < sections)
        count = count + there.astype(jnp.int32)

        @pl.when(there)
        def _(ds=ds):
            pl.semaphore_signal(barrier, inc=1, device_id={"section": sec + ds}, device_id_type=MESH)

    pl.semaphore_wait(barrier, count)

    def edge_copy(e, d):
        dr, dc = DIRECTIONS[d]
        if dc == 0:
            src, dst = out_row.at[e, (dr + 1) // 2], halo_row.at[e, (1 - dr) // 2]
        elif dr == 0:
            src, dst = out_col.at[e, (dc + 1) // 2], halo_col.at[e, (1 - dc) // 2]
        else:
            start = 0 if dr < 0 else height - 8
            src = out_col.at[e, (dc + 1) // 2, pl.ds(start, 8)]
            dst = halo_cor.at[e, (1 - dr) // 2, (1 - dc) // 2]
        return pltpu.make_async_remote_copy(
            src_ref=src, dst_ref=dst, send_sem=send_sem.at[e, d], recv_sem=recv_sem.at[e, d],
            device_id=target(dr, dc), device_id_type=MESH,
        )

    def send_edges(e, which):
        for d in which:
            @pl.when(exists(*DIRECTIONS[d]))
            def _(d=d):
                edge_copy(e, d).start()

    def receive_edges(e):
        for d, (dr, dc) in enumerate(DIRECTIONS):
            @pl.when(exists(-dr, -dc))
            def _(d=d):
                edge_copy(e, d).wait_recv()

    def column(shape):
        return lax.broadcasted_iota(jnp.int32, shape, 1)

    def put(stk, at, values, left, right):
        n = values.shape[0]
        at_col = column(values.shape)
        stk[pl.ds(at, n), :, chan : 2 * chan] = values.astype(jnp.bfloat16)
        stk[pl.ds(at, n), :, :chan] = jnp.where(
            at_col == 0, left, pltpu.roll(values, 1, 1)).astype(jnp.bfloat16)
        stk[pl.ds(at, n), :, 2 * chan :] = jnp.where(
            at_col == width - 1, right, pltpu.roll(values, width - 1, 1)).astype(jnp.bfloat16)

    def put_main(e, stk, start, values):
        put(stk, start + 1, values, 0.0, 0.0)
        rows = pl.ds(pl.multiple_of(start, CHUNK), CHUNK)
        out_col[e, 0, rows] = values[:, 0, :]
        out_col[e, 1, rows] = values[:, width - 1, :]

    def finish(e, stk):
        receive_edges(e)
        for side in range(2):
            at = 0 if side == 0 else height + 1
            line = 7 if side == 0 else 0
            put(
                stk, at, halo_row[e, side].astype(jnp.float32)[None],
                halo_cor[e, side, 0][line : line + 1][None],
                halo_cor[e, side, 1][line : line + 1][None],
            )

        @pl.loop(0, chunks)
        def _(k):
            start = pl.multiple_of(k * CHUNK, CHUNK)
            for side in range(2):
                part = pl.ds(0, 16) if side == 0 else pl.ds(width - 16, 16)
                lanes = pl.ds(2 * chan * side, chan)
                old = stk[pl.ds(start + 1, CHUNK), part, lanes].astype(jnp.float32)
                edge = halo_col[e, side, pl.ds(start, CHUNK)].reshape(CHUNK, 1, chan)
                stk[pl.ds(start + 1, CHUNK), part, lanes] = jnp.where(
                    column(old.shape) == 15 * side, edge, old).astype(jnp.bfloat16)

    def conv(stk, w, start):
        total = None
        for tap in range(3):
            part = stk[pl.ds(start + tap, CHUNK)].reshape(CHUNK * width, 3 * chan)
            dot = jnp.dot(part, w[tap], preferred_element_type=jnp.float32)
            total = dot if total is None else total + dot
        return total

    def section_copy(k):
        rows = pl.ds(k * CHUNK, CHUNK)
        return pltpu.make_async_remote_copy(
            src_ref=out0.at[rows], dst_ref=x1.at[rows],
            send_sem=sec_send.at[k], recv_sem=sec_recv.at[k],
            device_id={"section": sec + 1}, device_id_type=MESH,
        )

    def result_copy(tick, k):
        rows = pl.ds(k * CHUNK, CHUNK)
        src = out0 if tick == 0 else out1
        return pltpu.make_async_copy(src.at[rows], out.at[tick, rows], out_sem.at[tick, k])

    for tick in range(TICKS):
        x = x0 if tick == 0 else x1
        e = 2 * tick
        if tick == 0:
            ins[0].wait()
        else:
            @pl.when(sec == 0)
            def _():
                fresh_copy.wait()

        @pl.loop(0, chunks)
        def _(k):
            if tick > 0:
                @pl.when(sec > 0)
                def _():
                    section_copy(k).wait_recv()
            put_main(e, stk_x, k * CHUNK, x[pl.ds(k * CHUNK, CHUNK)].astype(jnp.float32))

        out_row[e, 0] = x[0]
        out_row[e, 1] = x[height - 1]
        send_edges(e, range(8))
        if tick == 0:
            ins[1].wait()
        finish(e, stk_x)

        @pl.loop(0, chunks)
        def _(k):
            total = conv(stk_x, w1, k * CHUNK)
            hidden = jnp.maximum(gains[0:1] * total + shifts[0:1], 0.0)
            hidden = hidden.astype(jnp.bfloat16).astype(jnp.float32)
            put_main(e + 1, stk_h, k * CHUNK, hidden.reshape(CHUNK, width, chan))

        out_row[e + 1, 0] = stk_h[1, :, chan : 2 * chan]
        out_row[e + 1, 1] = stk_h[height, :, chan : 2 * chan]
        send_edges(e + 1, range(8))
        if tick == 0:
            ins[2].wait()
        finish(e + 1, stk_h)

        @pl.loop(0, chunks)
        def _(k):
            total = gains[1:2] * conv(stk_h, w2, k * CHUNK) + shifts[1:2]
            rows = pl.ds(k * CHUNK, CHUNK)
            summed = x[rows].astype(jnp.float32) + total.reshape(CHUNK, width, chan)
            result = out0 if tick == 0 else out1
            result[rows] = jnp.maximum(summed, 0.0).astype(jnp.bfloat16)
            if tick == 0:
                @pl.when(sec + 1 < sections)
                def _():
                    section_copy(k).start()
            result_copy(tick, k).start()

    for tick in range(TICKS):
        @pl.loop(0, chunks)
        def _(k):
            result_copy(tick, k).wait()

    @pl.when(sec + 1 < sections)
    def _():
        @pl.loop(0, chunks)
        def _(k):
            section_copy(k).wait_send()

    for e in range(2 * TICKS):
        for d, (dr, dc) in enumerate(DIRECTIONS):
            @pl.when(exists(dr, dc))
            def _(e=e, d=d):
                edge_copy(e, d).wait_send()


def per_device(sizes, state, fresh, conv_first, conv_second, gains, shifts):
    height, width, chan = fresh.shape
    chunks = height // CHUNK
    first = conv_first[0].reshape(3, 3 * chan, chan)
    second = conv_second[0].reshape(3, 3 * chan, chan)
    steps = 2 * TICKS
    tile = pltpu.VMEM((height, width, chan), jnp.bfloat16)
    weight = pltpu.VMEM((3, 3 * chan, chan), jnp.bfloat16)
    stack = pltpu.VMEM((height + 2, width, 3 * chan), jnp.bfloat16)
    anywhere = pl.BlockSpec(memory_space=pl.ANY)
    in_vmem = pl.BlockSpec(memory_space=pltpu.VMEM)
    result = pl.pallas_call(
        functools.partial(kernel, *sizes),
        out_shape=jax.ShapeDtypeStruct((TICKS, height, width, chan), jnp.bfloat16),
        in_specs=[anywhere] * 4 + [in_vmem] * 2,
        out_specs=anywhere,
        scratch_shapes=[
            tile, tile, tile, tile, weight, weight, stack, stack,
            pltpu.VMEM((steps, 2, width, chan), jnp.bfloat16),
            pltpu.VMEM((steps, 2, height, chan), jnp.float32),
            pltpu.VMEM((steps, 2, width, chan), jnp.bfloat16),
            pltpu.VMEM((steps, 2, height, chan), jnp.float32),
            pltpu.VMEM((steps, 2, 2, 8, chan), jnp.float32),
            pltpu.SemaphoreType.DMA((4,)),
            pltpu.SemaphoreType.DMA((TICKS, chunks)),
            pltpu.SemaphoreType.DMA((steps, 8)),
            pltpu.SemaphoreType.DMA((steps, 8)),
            pltpu.SemaphoreType.DMA((chunks,)),
            pltpu.SemaphoreType.DMA((chunks,)),
        ],
        compiler_params=pltpu.CompilerParams(
            collective_id=0, has_side_effects=True, vmem_limit_bytes=40 * 1024 * 1024
        ),
    )(state[0], fresh, first, second, gains[0], shifts[0])
    return result[:, None]


def solution(mesh):
    sizes = tuple(mesh.shape[axis] for axis in ("section", "row", "col"))
    in_specs = (
        P("section", "row", "col", None),
        P("row", "col", None),
        P("section", None, None, None, None),
        P("section", None, None, None, None),
        P("section", None, None),
        P("section", None, None),
    )
    out_specs = P(None, "section", "row", "col", None)
    return jax.shard_map(
        functools.partial(per_device, sizes),
        mesh=mesh, in_specs=in_specs, out_specs=out_specs, check_vma=False,
    )
```

time: 97.4 us -> 43.7 us (0.45)
  Pallas kernels: 0 us -> 36.5 us
  waiting for transfers between devices: 36.4 us -> 0 us
  starting transfers between devices: 36.1 us -> 0 us
  other arithmetic: 11.6 us -> 0 us
  matrix products: 7.04 us -> 0 us
  local copies, waits for them, and re-layouts: 4.97 us -> 6.96 us
    pallas_call x0 -> x1, Pallas kernels: none -> 36.5 us  [per_device(): pl.pallas_call(functools.partial(kernel, *sizes), out_shape=jax.ShapeDtyp...]
    ppermute x17 -> x0, waiting for transfers between devices: 36.4 us -> none  [the longest x8 23.6 us: extended(): lax.ppermute(lax.slice_in_dim(block, 0, width, axis=dim), axis, backward)]
    ppermute x17 -> x0, starting transfers between devices: 36.1 us -> none  [the longest x8 19.4 us: extended(): lax.ppermute(lax.slice_in_dim(block, block.shape[dim] - width, None, axis...]
    concatenate x4 -> x0, other arithmetic: 7.44 us -> none  [convolve(): jnp.concatenate([padded[:, col_tap:col_tap + out_cols] for col_tap in ran...]
    dot_general x12 -> x0, matrix products: 7.04 us -> none  [convolve(): jnp.dot(stacked[row_tap:row_tap + out_rows].reshape(out_rows * out_cols,...]
    unnamed x12 -> x13, local copies, waits for them, and re-layouts: 0.42 us -> 6.96 us
    slice x12 -> x0, local copies, waits for them, and re-layouts: 4.55 us -> none  [the longest x4 2.33 us: convolve(): stacked[row_tap:row_tap + out_rows]]
    convert_element_type x4 -> x0, other arithmetic: 1.5 us -> none  [the longest x2 1.22 us: section_block(): return jax.nn.relu(summed).astype(jnp.bfloat16)]
  transfers between devices with their start and end apart: 17 -> 0, of which waited for: 9 -> 0; matrix products, arithmetic and copies ran while one was open for 2% -> 0% of each run, Pallas kernels for 0% -> 0%
where the time goes in v1:
time: 43.7 us; the launch traced here: 43.4 us
  Pallas kernels  36.5 us (84%)
  local copies, waits for them, and re-layouts  6.96 us (16%)
    pallas_call x1, Pallas kernels, per_device(): pl.pallas_call(functools.partial(kernel, *sizes), out_shape=jax.ShapeDtyp...  36.5 us
    unnamed x13, local copies, waits for them, and re-layouts  6.96 us

profile of v1, /device:TPU:17, one launch (start us, length us, event | category | flops | bytes accessed | tf_op | source)
XLA Modules:
  0.0 43.4 jit_solution(4686041306218638230)
XLA Ops:
  0.0 0.0 copy-start
  0.0 1.3 %copy-done = bf16[1,3,3,256,256]{4,3,2,1,0:T(8,128)(2,1)S(1)} copy-done((bf16[1,3,3,256,256]{4,3,2,1,0:T(8,128)(2,1)S(1)}, bf16[1,3,3,256,256]{4,3,2,1,0:T(8,128)(2,1)}, u32[]{:S(2)}) %copy-start) | copy-done | bytes 1179672
  1.3 0.0 copy-start.1
  1.3 1.3 %copy-done.1 = bf16[1,3,3,256,256]{4,3,2,1,0:T(8,128)(2,1)S(1)} copy-done((bf16[1,3,3,256,256]{4,3,2,1,0:T(8,128)(2,1)S(1)}, bf16[1,3,3,256,256]{4,3,2,1,0:T(8,128)(2,1)}, u32[]{:S(2)}) %copy-start.1) | copy-done | bytes 1179672
  2.5 0.0 copy-start.2
  2.5 1.0 %copy-done.2 = bf16[1,32,32,256]{3,2,1,0:T(8,128)(2,1)S(1)} copy-done((bf16[1,32,32,256]{3,2,1,0:T(8,128)(2,1)S(1)}, bf16[1,32,32,256]{3,2,1,0:T(8,128)(2,1)}, u32[]{:S(2)}) %copy-start.2) | copy-done | bytes 524312
  3.6 0.0 copy-start.3
  3.6 1.0 %copy-done.3 = bf16[32,32,256]{2,1,0:T(8,128)(2,1)S(1)} copy-done((bf16[32,32,256]{2,1,0:T(8,128)(2,1)S(1)}, bf16[32,32,256]{2,1,0:T(8,128)(2,1)}, u32[]{:S(2)}) %copy-start.3) | copy-done | bytes 524312
  4.6 0.0 copy-start.4
  4.6 0.7 %copy-done.4 = f32[1,2,256]{2,1,0:T(2,128)S(1)} copy-done((f32[1,2,256]{2,1,0:T(2,128)S(1)}, f32[1,2,256]{2,1,0:T(2,128)}, u32[]{:S(2)}) %copy-start.4) | copy-done | bytes 2072
  5.3 0.0 copy-start.5
  5.3 0.7 %copy-done.5 = f32[1,2,256]{2,1,0:T(2,128)S(1)} copy-done((f32[1,2,256]{2,1,0:T(2,128)S(1)}, f32[1,2,256]{2,1,0:T(2,128)}, u32[]{:S(2)}) %copy-start.5) | copy-done | bytes 2072
  6.0 36.5 %shard_map.64 = bf16[2,32,32,256]{3,2,1,0:T(8,128)(2,1)S(1)} custom-call(bf16[32,32,256]{2,1,0:T(8,128)(2,1)S(1)} %bitcast.11, bf16[32,32,256]{2,1,0:T(8,128)(2,1)S(1)} %copy-done.3, bf16[3,768,256]{2,1,0:T(8,128)(2,1)S(1)} %bitcast.9, bf16[3,768,256]{2,1,0:T(8,128)(2,1)S(1)} %bitcast.10, f32[2,256]{1,0:T(2,128)S(1)} %bitcast.12, f32[2,256]{1,0:T(2,128)S(1)} %bitcast.13), custom_call_target="tpu_custom_call" | custom-call | tf_op jit(solution)/shard_map/pallas_call | solution.py:241
  42.4 1.0 %copy.9 = bf16[2,1,32,32,256]{4,3,2,1,0:T(8,128)(2,1)} copy(bf16[2,1,32,32,256]{4,3,2,1,0:T(8,128)(2,1)S(1)} %bitcast.8) | data formatting | bytes 2097152
Async XLA Ops:
  0.0 1.3 %copy-start = (bf16[1,3,3,256,256]{4,3,2,1,0:T(8,128)(2,1)S(1)}, bf16[1,3,3,256,256]{4,3,2,1,0:T(8,128)(2,1)}, u32[]{:S(2)}) copy-start(bf16[1,3,3,256,256]{4,3,2,1,0:T(8,128)(2,1)} %param.8) | copy-start | bytes 3538948
  1.3 1.3 %copy-start.1 = (bf16[1,3,3,256,256]{4,3,2,1,0:T(8,128)(2,1)S(1)}, bf16[1,3,3,256,256]{4,3,2,1,0:T(8,128)(2,1)}, u32[]{:S(2)}) copy-start(bf16[1,3,3,256,256]{4,3,2,1,0:T(8,128)(2,1)} %param.9) | copy-start | bytes 3538948
  2.5 1.0 %copy-start.2 = (bf16[1,32,32,256]{3,2,1,0:T(8,128)(2,1)S(1)}, bf16[1,32,32,256]{3,2,1,0:T(8,128)(2,1)}, u32[]{:S(2)}) copy-start(bf16[1,32,32,256]{3,2,1,0:T(8,128)(2,1)} %param.6) | copy-start | bytes 1572868
  3.6 1.0 %copy-start.3 = (bf16[32,32,256]{2,1,0:T(8,128)(2,1)S(1)}, bf16[32,32,256]{2,1,0:T(8,128)(2,1)}, u32[]{:S(2)}) copy-start(bf16[32,32,256]{2,1,0:T(8,128)(2,1)} %fresh.1) | copy-start | bytes 1572868
  4.6 0.7 %copy-start.4 = (f32[1,2,256]{2,1,0:T(2,128)S(1)}, f32[1,2,256]{2,1,0:T(2,128)}, u32[]{:S(2)}) copy-start(f32[1,2,256]{2,1,0:T(2,128)} %param.10) | copy-start | bytes 6148
  5.3 0.7 %copy-start.5 = (f32[1,2,256]{2,1,0:T(2,128)S(1)}, f32[1,2,256]{2,1,0:T(2,128)}, u32[]{:S(2)}) copy-start(f32[1,2,256]{2,1,0:T(2,128)} %param.11) | copy-start | bytes 6148

commit v2 on v1

v2 whole, which is shorter than its diff:
```python
import functools

import jax
import jax.numpy as jnp
from jax import lax
from jax.experimental import pallas as pl
from jax.experimental.pallas import tpu as pltpu
from jax.sharding import PartitionSpec as P

TICKS = 2
CHUNK = 8
DIRECTIONS = ((-1, 0), (1, 0), (0, -1), (0, 1), (-1, -1), (-1, 1), (1, -1), (1, 1))
MESH = pl.DeviceIdType.MESH


def kernel(
    sections, rows_n, cols_n,
    state, fresh, first, second, gains_in, shifts_in, out,
    gains, shifts, x0, x1, out0, out1, w1, w2, stk_x, stk_h,
    out_row, out_col, halo_row, halo_col, halo_cor,
    in_sem, out_sem, send_sem, recv_sem, col_send, col_recv, sec_send, sec_recv,
):
    height, width, chan = x0.shape
    chunks = height // CHUNK
    sec = lax.axis_index("section")
    row = lax.axis_index("row")
    col = lax.axis_index("col")

    def exists(dr, dc):
        return (row + dr >= 0) & (row + dr < rows_n) & (col + dc >= 0) & (col + dc < cols_n)

    def target(dr, dc):
        return {"row": row + dr, "col": col + dc}

    copies = [
        pltpu.make_async_copy(src, dst, in_sem.at[n])
        for n, (src, dst) in enumerate(
            ((state, x0), (first, w1), (gains_in, gains), (shifts_in, shifts), (second, w2))
        )
    ]
    fresh_copy = pltpu.make_async_copy(fresh, x1, in_sem.at[5])
    for copy in copies:
        copy.start()

    @pl.when(sec == 0)
    def _():
        fresh_copy.start()

    halo_row[...] = jnp.zeros_like(halo_row)
    halo_col[...] = jnp.zeros_like(halo_col)
    halo_cor[...] = jnp.zeros_like(halo_cor)

    barrier = pltpu.get_barrier_semaphore()
    count = jnp.int32(0)
    for dr, dc in DIRECTIONS:
        there = exists(dr, dc)
        count = count + there.astype(jnp.int32)

        @pl.when(there)
        def _(dr=dr, dc=dc):
            pl.semaphore_signal(barrier, inc=1, device_id=target(dr, dc), device_id_type=MESH)

    for ds in (-1, 1):
        there = (sec + ds >= 0) & (sec + ds < sections)
        count = count + there.astype(jnp.int32)

        @pl.when(there)
        def _(ds=ds):
            pl.semaphore_signal(barrier, inc=1, device_id={"section": sec + ds}, device_id_type=MESH)

    def edge_copy(e, d):
        dr, dc = DIRECTIONS[d]
        if dc == 0:
            src, dst = out_row.at[e, (dr + 1) // 2], halo_row.at[e, (1 - dr) // 2]
        else:
            start = 0 if dr < 0 else height - 8
            src = out_col.at[e, (dc + 1) // 2, pl.ds(start, 8)]
            dst = halo_cor.at[e, (1 - dr) // 2, (1 - dc) // 2]
        return pltpu.make_async_remote_copy(
            src_ref=src, dst_ref=dst, send_sem=send_sem.at[e, d], recv_sem=recv_sem.at[e, d],
            device_id=target(dr, dc), device_id_type=MESH,
        )

    def col_copy(e, side, k):
        rows = pl.ds(pl.multiple_of(k * CHUNK, CHUNK), CHUNK)
        return pltpu.make_async_remote_copy(
            src_ref=out_col.at[e, side, rows], dst_ref=halo_col.at[e, 1 - side, rows],
            send_sem=col_send.at[e, side, k], recv_sem=col_recv.at[e, side, k],
            device_id=target(0, 2 * side - 1), device_id_type=MESH,
        )

    def send_rows(e, way):
        for d, (dr, dc) in enumerate(DIRECTIONS):
            if dr == way:
                @pl.when(exists(dr, dc))
                def _(d=d):
                    edge_copy(e, d).start()

    def send(e, k):
        for side in range(2):
            @pl.when(exists(0, 2 * side - 1))
            def _(side=side):
                col_copy(e, side, k).start()

        @pl.when(k == 0)
        def _():
            send_rows(e, -1)

        @pl.when(k == chunks - 1)
        def _():
            send_rows(e, 1)

    def column(shape):
        return lax.broadcasted_iota(jnp.int32, shape, 1)

    def put(stk, at, values, left, right):
        n = values.shape[0]
        at_col = column(values.shape)
        stk[pl.ds(at, n), :, chan : 2 * chan] = values.astype(jnp.bfloat16)
        stk[pl.ds(at, n), :, :chan] = jnp.where(
            at_col == 0, left, pltpu.roll(values, 1, 1)).astype(jnp.bfloat16)
        stk[pl.ds(at, n), :, 2 * chan :] = jnp.where(
            at_col == width - 1, right, pltpu.roll(values, width - 1, 1)).astype(jnp.bfloat16)

    def put_main(e, stk, start, values):
        put(stk, start + 1, values, 0.0, 0.0)
        rows = pl.ds(pl.multiple_of(start, CHUNK), CHUNK)
        out_col[e, 0, rows] = values[:, 0, :]
        out_col[e, 1, rows] = values[:, width - 1, :]

    def fix_row(e, stk, side):
        for d, (dr, dc) in enumerate(DIRECTIONS):
            if dr == 1 - 2 * side:
                @pl.when(exists(-dr, -dc))
                def _(d=d):
                    edge_copy(e, d).wait_recv()
        at = 0 if side == 0 else height + 1
        line = 7 if side == 0 else 0
        put(
            stk, at, halo_row[e, side].astype(jnp.float32)[None],
            halo_cor[e, side, 0][line : line + 1][None],
            halo_cor[e, side, 1][line : line + 1][None],
        )

    def fix(e, stk, k):
        start = pl.multiple_of(k * CHUNK, CHUNK)
        for side in range(2):
            @pl.when(exists(0, 2 * side - 1))
            def _(side=side):
                col_copy(e, 1 - side, k).wait_recv()
                part = pl.ds(0, 16) if side == 0 else pl.ds(width - 16, 16)
                lanes = pl.ds(2 * chan * side, chan)
                old = stk[pl.ds(start + 1, CHUNK), part, lanes].astype(jnp.float32)
                edge = halo_col[e, side, pl.ds(start, CHUNK)].reshape(CHUNK, 1, chan)
                stk[pl.ds(start + 1, CHUNK), part, lanes] = jnp.where(
                    column(old.shape) == 15 * side, edge, old).astype(jnp.bfloat16)

        @pl.when(k == 0)
        def _():
            fix_row(e, stk, 0)

        @pl.when(k == chunks - 1)
        def _():
            fix_row(e, stk, 1)

    def conv(stk, w, start):
        total = None
        for tap in range(3):
            part = stk[pl.ds(start + tap, CHUNK)].reshape(CHUNK * width, 3 * chan)
            dot = jnp.dot(part, w[tap], preferred_element_type=jnp.float32)
            total = dot if total is None else total + dot
        return total

    def section_copy(k):
        rows = pl.ds(k * CHUNK, CHUNK)
        return pltpu.make_async_remote_copy(
            src_ref=out0.at[rows], dst_ref=x1.at[rows],
            send_sem=sec_send.at[k], recv_sem=sec_recv.at[k],
            device_id={"section": sec + 1}, device_id_type=MESH,
        )

    def result_copy(tick, k):
        rows = pl.ds(k * CHUNK, CHUNK)
        src = out0 if tick == 0 else out1
        return pltpu.make_async_copy(src.at[rows], out.at[tick, rows], out_sem.at[tick, k])

    def load(tick, k):
        x = x0 if tick == 0 else x1
        e = 2 * tick
        put_main(e, stk_x, k * CHUNK, x[pl.ds(k * CHUNK, CHUNK)].astype(jnp.float32))

        @pl.when(k == 0)
        def _():
            out_row[e, 0] = x[0]

        @pl.when(k == chunks - 1)
        def _():
            out_row[e, 1] = x[height - 1]

    def first_conv(tick, k):
        e = 2 * tick + 1
        total = conv(stk_x, w1, k * CHUNK)
        hidden = jnp.maximum(gains[0:1] * total + shifts[0:1], 0.0)
        hidden = hidden.astype(jnp.bfloat16).astype(jnp.float32)
        put_main(e, stk_h, k * CHUNK, hidden.reshape(CHUNK, width, chan))

        @pl.when(k == 0)
        def _():
            out_row[e, 0] = stk_h[1, :, chan : 2 * chan]

        @pl.when(k == chunks - 1)
        def _():
            out_row[e, 1] = stk_h[height, :, chan : 2 * chan]

        send(e, k)

    def second_conv(tick, k):
        x = x0 if tick == 0 else x1
        total = gains[1:2] * conv(stk_h, w2, k * CHUNK) + shifts[1:2]
        rows = pl.ds(k * CHUNK, CHUNK)
        summed = x[rows].astype(jnp.float32) + total.reshape(CHUNK, width, chan)
        result = out0 if tick == 0 else out1
        result[rows] = jnp.maximum(summed, 0.0).astype(jnp.bfloat16)
        if tick == 0:
            @pl.when(sec + 1 < sections)
            def _():
                section_copy(k).start()
        result_copy(tick, k).start()

    copies[0].wait()

    @pl.loop(0, chunks)
    def _(k):
        load(0, k)

    pl.semaphore_wait(barrier, count)

    @pl.loop(0, chunks)
    def _(k):
        send(0, k)

    for copy in copies[1:]:
        copy.wait()

    for tick in range(TICKS):
        if tick > 0:
            @pl.when(sec == 0)
            def _():
                fresh_copy.wait()

        @pl.loop(0 if tick else 1, chunks + 4)
        def _(i, tick=tick):
            if tick > 0:
                @pl.when(i < chunks)
                def _():
                    @pl.when(sec > 0)
                    def _():
                        section_copy(i).wait_recv()
                    load(tick, i)
                    send(2 * tick, i)

            @pl.when((i >= 1) & (i < chunks + 1))
            def _():
                fix(2 * tick, stk_x, i - 1)

            @pl.when((i >= 2) & (i < chunks + 2))
            def _():
                first_conv(tick, i - 2)

            @pl.when((i >= 3) & (i < chunks + 3))
            def _():
                fix(2 * tick + 1, stk_h, i - 3)

            @pl.when(i >= 4)
            def _():
                second_conv(tick, i - 4)

    for tick in range(TICKS):
        @pl.loop(0, chunks)
        def _(k):
            result_copy(tick, k).wait()

    @pl.when(sec + 1 < sections)
    def _():
        @pl.loop(0, chunks)
        def _(k):
            section_copy(k).wait_send()

    for e in range(2 * TICKS):
        for d, (dr, dc) in enumerate(DIRECTIONS):
            @pl.when(exists(dr, dc))
            def _(e=e, d=d, dr=dr, dc=dc):
                if dr != 0:
                    edge_copy(e, d).wait_send()
                else:
                    @pl.loop(0, chunks)
                    def _(k):
                        col_copy(e, (dc + 1) // 2, k).wait_send()


def per_device(sizes, state, fresh, conv_first, conv_second, gains, shifts):
    height, width, chan = fresh.shape
    chunks = height // CHUNK
    first = conv_first[0].reshape(3, 3 * chan, chan)
    second = conv_second[0].reshape(3, 3 * chan, chan)
    steps = 2 * TICKS
    tile = pltpu.VMEM((height, width, chan), jnp.bfloat16)
    weight = pltpu.VMEM((3, 3 * chan, chan), jnp.bfloat16)
    stack = pltpu.VMEM((height + 2, width, 3 * chan), jnp.bfloat16)
    scale = pltpu.VMEM(gains.shape[1:], jnp.float32)
    anywhere = pl.BlockSpec(memory_space=pl.ANY)
    result = pl.pallas_call(
        functools.partial(kernel, *sizes),
        out_shape=jax.ShapeDtypeStruct((TICKS, height, width, chan), jnp.bfloat16),
        in_specs=[anywhere] * 6,
        out_specs=anywhere,
        scratch_shapes=[
            scale, scale, tile, tile, tile, tile, weight, weight, stack, stack,
            pltpu.VMEM((steps, 2, width, chan), jnp.bfloat16),
            pltpu.VMEM((steps, 2, height, chan), jnp.float32),
            pltpu.VMEM((steps, 2, width, chan), jnp.bfloat16),
            pltpu.VMEM((steps, 2, height, chan), jnp.float32),
            pltpu.VMEM((steps, 2, 2, 8, chan), jnp.float32),
            pltpu.SemaphoreType.DMA((6,)),
            pltpu.SemaphoreType.DMA((TICKS, chunks)),
            pltpu.SemaphoreType.DMA((steps, 8)),
            pltpu.SemaphoreType.DMA((steps, 8)),
            pltpu.SemaphoreType.DMA((steps, 2, chunks)),
            pltpu.SemaphoreType.DMA((steps, 2, chunks)),
            pltpu.SemaphoreType.DMA((chunks,)),
            pltpu.SemaphoreType.DMA((chunks,)),
        ],
        compiler_params=pltpu.CompilerParams(
            collective_id=0, has_side_effects=True, vmem_limit_bytes=62 * 1024 * 1024
        ),
    )(state[0], fresh, first, second, gains[0], shifts[0])
    return result[:, None]


def solution(mesh):
    sizes = tuple(mesh.shape[axis] for axis in ("section", "row", "col"))
    in_specs = (
        P("section", "row", "col", None),
        P("row", "col", None),
        P("section", None, None, None, None),
        P("section", None, None, None, None),
        P("section", None, None),
        P("section", None, None),
    )
    out_specs = P(None, "section", "row", "col", None)
    return jax.shard_map(
        functools.partial(per_device, sizes),
        mesh=mesh, in_specs=in_specs, out_specs=out_specs, check_vma=False,
    )
```

time: 43.7 us -> 45.8 us (1.048)
  the two profiles are of different devices: /device:TPU:17 before, /device:TPU:19 now
where the time goes in v2:
time: 45.8 us; the launch traced here: 45.7 us
  Pallas kernels  43.4 us (95%)
  local copies, waits for them, and re-layouts  2.26 us (5%)
    pallas_call x1, Pallas kernels, per_device(): pl.pallas_call(functools.partial(kernel, *sizes), out_shape=jax.ShapeDtyp...  43.4 us
    unnamed x1, local copies, waits for them, and re-layouts  2.26 us

profile of v2, /device:TPU:19, one launch (start us, length us, event | category | flops | bytes accessed | tf_op | source)
XLA Modules:
  0.0 45.7 jit_solution(11768391951189057215)
XLA Ops:
  0.0 43.4 %shard_map.64 = bf16[2,32,32,256]{3,2,1,0:T(8,128)(2,1)} custom-call(bf16[32,32,256]{2,1,0:T(8,128)(2,1)} %bitcast.11, bf16[32,32,256]{2,1,0:T(8,128)(2,1)} %fresh.1, bf16[3,768,256]{2,1,0:T(8,128)(2,1)} %bitcast.9, bf16[3,768,256]{2,1,0:T(8,128)(2,1)} %bitcast.10, f32[2,256]{1,0:T(2,128)} %bitcast.12, f32[2,256]{1,0:T(2,128)} %bitcast.13), custom_call_target="tpu_custom_call" | custom-call | tf_op jit(solution)/shard_map/pallas_call | solution.py:312
  43.4 2.3 %copy.9 = bf16[2,1,32,32,256]{4,3,2,1,0:T(8,128)(2,1)} copy(bf16[2,1,32,32,256]{4,3,2,1,0:T(8,128)(2,1)} %bitcast.8) | data formatting | bytes 2097152

commit v3 on v2

--- a/solution.py
+++ b/solution.py
@@ -26,6 +26,14 @@
     row = lax.axis_index("row")
     col = lax.axis_index("col")
 
+    def when(condition):
+        if isinstance(condition, bool):
+            return lambda f: f() if condition else None
+        return pl.when(condition)
+
+    def start_of(k):
+        return k * CHUNK if isinstance(k, int) else pl.multiple_of(k * CHUNK, CHUNK)
+
     def exists(dr, dc):
         return (row + dr >= 0) & (row + dr < rows_n) & (col + dc >= 0) & (col + dc < cols_n)
 
@@ -82,7 +90,7 @@
         )
 
     def col_copy(e, side, k):
-        rows = pl.ds(pl.multiple_of(k * CHUNK, CHUNK), CHUNK)
+        rows = pl.ds(start_of(k), CHUNK)
         return pltpu.make_async_remote_copy(
             src_ref=out_col.at[e, side, rows], dst_ref=halo_col.at[e, 1 - side, rows],
             send_sem=col_send.at[e, side, k], recv_sem=col_recv.at[e, side, k],
@@ -102,11 +110,11 @@
             def _(side=side):
                 col_copy(e, side, k).start()
 
-        @pl.when(k == 0)
+        @when(k == 0)
         def _():
             send_rows(e, -1)
 
-        @pl.when(k == chunks - 1)
+        @when(k == chunks - 1)
         def _():
             send_rows(e, 1)
 
@@ -124,7 +132,7 @@
 
     def put_main(e, stk, start, values):
         put(stk, start + 1, values, 0.0, 0.0)
-        rows = pl.ds(pl.multiple_of(start, CHUNK), CHUNK)
+        rows = pl.ds(start_of(start // CHUNK) if isinstance(start, int) else pl.multiple_of(start, CHUNK), CHUNK)
         out_col[e, 0, rows] = values[:, 0, :]
         out_col[e, 1, rows] = values[:, width - 1, :]
 
@@ -143,7 +151,7 @@
         )
 
     def fix(e, stk, k):
-        start = pl.multiple_of(k * CHUNK, CHUNK)
+        start = start_of(k)
         for side in range(2):
             @pl.when(exists(0, 2 * side - 1))
             def _(side=side):
@@ -155,11 +163,11 @@
                 stk[pl.ds(start + 1, CHUNK), part, lanes] = jnp.where(
                     column(old.shape) == 15 * side, edge, old).astype(jnp.bfloat16)
 
-        @pl.when(k == 0)
+        @when(k == 0)
         def _():
             fix_row(e, stk, 0)
 
-        @pl.when(k == chunks - 1)
+        @when(k == chunks - 1)
         def _():
             fix_row(e, stk, 1)
 
@@ -189,11 +197,11 @@
         e = 2 * tick
         put_main(e, stk_x, k * CHUNK, x[pl.ds(k * CHUNK, CHUNK)].astype(jnp.float32))
 
-        @pl.when(k == 0)
+        @when(k == 0)
         def _():
             out_row[e, 0] = x[0]
 
-        @pl.when(k == chunks - 1)
+        @when(k == chunks - 1)
         def _():
             out_row[e, 1] = x[height - 1]
 
@@ -204,11 +212,11 @@
         hidden = hidden.astype(jnp.bfloat16).astype(jnp.float32)
         put_main(e, stk_h, k * CHUNK, hidden.reshape(CHUNK, width, chan))
 
-        @pl.when(k == 0)
+        @when(k == 0)
         def _():
             out_row[e, 0] = stk_h[1, :, chan : 2 * chan]
 
-        @pl.when(k == chunks - 1)
+        @when(k == chunks - 1)
         def _():
             out_row[e, 1] = stk_h[height, :, chan : 2 * chan]
 
@@ -242,38 +250,46 @@
     for copy in copies[1:]:
         copy.wait()
 
+    last = chunks - 1
+    order = [0, last] + list(range(1, last))
     for tick in range(TICKS):
-        if tick > 0:
+        fixed, done = set(), set()
+
+        def ready(k):
+            return all(n in done for n in (k - 1, k, k + 1) if 0 <= n < chunks)
+
+        def need(e, stk, k):
+            for n in (k - 1, k, k + 1):
+                if 0 <= n < chunks and (e, n) not in fixed:
+                    fixed.add((e, n))
+                    fix(e, stk, n)
+
+        todo = list(order)
+        if tick == 0:
+            done.update(order)
+        else:
             @pl.when(sec == 0)
             def _():
                 fresh_copy.wait()
 
-        @pl.loop(0 if tick else 1, chunks + 4)
-        def _(i, tick=tick):
-            if tick > 0:
-                @pl.when(i < chunks)
-                def _():
-                    @pl.when(sec > 0)
-                    def _():
-                        section_copy(i).wait_recv()
-                    load(tick, i)
-                    send(2 * tick, i)
-
-            @pl.when((i >= 1) & (i < chunks + 1))
-            def _():
-                fix(2 * tick, stk_x, i - 1)
-
-            @pl.when((i >= 2) & (i < chunks + 2))
-            def _():
-                first_conv(tick, i - 2)
-
-            @pl.when((i >= 3) & (i < chunks + 3))
-            def _():
-                fix(2 * tick + 1, stk_h, i - 3)
-
-            @pl.when(i >= 4)
-            def _():
-                second_conv(tick, i - 4)
+            for k in order:
+                if k == order[-1] and ready(0):
+                    need(2, stk_x, 0)
+                    first_conv(tick, 0)
+                    todo.remove(0)
+
+                @pl.when(sec > 0)
+                def _(k=k):
+                    section_copy(k).wait_recv()
+                load(tick, k)
+                send(2, k)
+                done.add(k)
+        for k in todo:
+            need(2 * tick, stk_x, k)
+            first_conv(tick, k)
+        for k in order:
+            need(2 * tick + 1, stk_h, k)
+            second_conv(tick, k)
 
     for tick in range(TICKS):
         @pl.loop(0, chunks)

time: 45.8 us -> 38.6 us (0.84)
  the two profiles are of different devices: /device:TPU:19 before, /device:TPU:17 now
where the time goes in v3:
time: 38.6 us; the launch traced here: 37.9 us
  Pallas kernels  35.6 us (92%)
  local copies, waits for them, and re-layouts  2.26 us (6%)
    pallas_call x1, Pallas kernels, per_device(): pl.pallas_call(functools.partial(kernel, *sizes), out_shape=jax.ShapeDtyp...  35.6 us
    unnamed x1, local copies, waits for them, and re-layouts  2.26 us

profile of v3, /device:TPU:17, one launch (start us, length us, event | category | flops | bytes accessed | tf_op | source)
XLA Modules:
  0.0 37.9 jit_solution(9154046038802610973)
XLA Ops:
  0.0 35.6 %shard_map.64 = bf16[2,32,32,256]{3,2,1,0:T(8,128)(2,1)} custom-call(bf16[32,32,256]{2,1,0:T(8,128)(2,1)} %bitcast.11, bf16[32,32,256]{2,1,0:T(8,128)(2,1)} %fresh.1, bf16[3,768,256]{2,1,0:T(8,128)(2,1)} %bitcast.9, bf16[3,768,256]{2,1,0:T(8,128)(2,1)} %bitcast.10, f32[2,256]{1,0:T(2,128)} %bitcast.12, f32[2,256]{1,0:T(2,128)} %bitcast.13), custom_call_target="tpu_custom_call" | custom-call | tf_op jit(solution)/shard_map/pallas_call | solution.py:328
  35.7 2.3 %copy.9 = bf16[2,1,32,32,256]{4,3,2,1,0:T(8,128)(2,1)} copy(bf16[2,1,32,32,256]{4,3,2,1,0:T(8,128)(2,1)} %bitcast.8) | data formatting | bytes 2097152

commit v4 on v3

--- a/solution.py
+++ b/solution.py
@@ -8,7 +8,7 @@
 from jax.sharding import PartitionSpec as P
 
 TICKS = 2
-CHUNK = 8
+CHUNK = 16
 DIRECTIONS = ((-1, 0), (1, 0), (0, -1), (0, 1), (-1, -1), (-1, 1), (1, -1), (1, 1))
 MESH = pl.DeviceIdType.MESH
 

time: 38.6 us -> 39.2 us (1.016); the launches traced: 37.9 us -> 39 us
  Pallas kernels: 35.6 us -> 36.7 us
    pallas_call x1, Pallas kernels: 35.6 us -> 36.7 us  [per_device(): pl.pallas_call(functools.partial(kernel, *sizes), out_shape=jax.ShapeDtyp...]
where the time goes in v4:
time: 39.2 us; the launch traced here: 39 us
  Pallas kernels  36.7 us (94%)
  local copies, waits for them, and re-layouts  2.26 us (6%)
    pallas_call x1, Pallas kernels, per_device(): pl.pallas_call(functools.partial(kernel, *sizes), out_shape=jax.ShapeDtyp...  36.7 us
    unnamed x1, local copies, waits for them, and re-layouts  2.26 us

profile of v4, /device:TPU:17, one launch (start us, length us, event | category | flops | bytes accessed | tf_op | source)
XLA Modules:
  0.0 39.0 jit_solution(11051328661432086922)
XLA Ops:
  0.0 36.7 %shard_map.64 = bf16[2,32,32,256]{3,2,1,0:T(8,128)(2,1)} custom-call(bf16[32,32,256]{2,1,0:T(8,128)(2,1)} %bitcast.11, bf16[32,32,256]{2,1,0:T(8,128)(2,1)} %fresh.1, bf16[3,768,256]{2,1,0:T(8,128)(2,1)} %bitcast.9, bf16[3,768,256]{2,1,0:T(8,128)(2,1)} %bitcast.10, f32[2,256]{1,0:T(2,128)} %bitcast.12, f32[2,256]{1,0:T(2,128)} %bitcast.13), custom_call_target="tpu_custom_call" | custom-call | tf_op jit(solution)/shard_map/pallas_call | solution.py:328
  36.7 2.3 %copy.9 = bf16[2,1,32,32,256]{4,3,2,1,0:T(8,128)(2,1)} copy(bf16[2,1,32,32,256]{4,3,2,1,0:T(8,128)(2,1)} %bitcast.8) | data formatting | bytes 2097152

commit v5 on v3

--- a/solution.py
+++ b/solution.py
@@ -247,7 +247,7 @@
     def _(k):
         send(0, k)
 
-    for copy in copies[1:]:
+    for copy in copies[1:4]:
         copy.wait()
 
     last = chunks - 1
@@ -284,10 +284,16 @@
                 load(tick, k)
                 send(2, k)
                 done.add(k)
+        early = tick == 0 and chunks > 3
         for k in todo:
             need(2 * tick, stk_x, k)
+            if tick == 0 and k == order[-1]:
+                copies[4].wait()
+                if early:
+                    need(1, stk_h, 0)
+                    second_conv(0, 0)
             first_conv(tick, k)
-        for k in order:
+        for k in order[1:] if early else order:
             need(2 * tick + 1, stk_h, k)
             second_conv(tick, k)
 

time: 38.6 us -> 39 us (1.010)
  Pallas kernels: 35.6 us -> 36 us
where the time goes in v5:
time: 39 us; the launch traced here: 38.3 us
  Pallas kernels  36 us (92%)
  local copies, waits for them, and re-layouts  2.26 us (6%)
    pallas_call x1, Pallas kernels, per_device(): pl.pallas_call(functools.partial(kernel, *sizes), out_shape=jax.ShapeDtyp...  36 us
    unnamed x1, local copies, waits for them, and re-layouts  2.26 us

profile of v5, /device:TPU:17, one launch (start us, length us, event | category | flops | bytes accessed | tf_op | source)
XLA Modules:
  0.0 38.3 jit_solution(12125308106641332103)
XLA Ops:
  0.0 36.0 %shard_map.64 = bf16[2,32,32,256]{3,2,1,0:T(8,128)(2,1)} custom-call(bf16[32,32,256]{2,1,0:T(8,128)(2,1)} %bitcast.11, bf16[32,32,256]{2,1,0:T(8,128)(2,1)} %fresh.1, bf16[3,768,256]{2,1,0:T(8,128)(2,1)} %bitcast.9, bf16[3,768,256]{2,1,0:T(8,128)(2,1)} %bitcast.10, f32[2,256]{1,0:T(2,128)} %bitcast.12, f32[2,256]{1,0:T(2,128)} %bitcast.13), custom_call_target="tpu_custom_call" | custom-call | tf_op jit(solution)/shard_map/pallas_call | solution.py:334
  36.0 2.3 %copy.9 = bf16[2,1,32,32,256]{4,3,2,1,0:T(8,128)(2,1)} copy(bf16[2,1,32,32,256]{4,3,2,1,0:T(8,128)(2,1)} %bitcast.8) | data formatting | bytes 2097152

commit v6 on v3

--- a/solution.py
+++ b/solution.py
@@ -133,8 +133,12 @@
     def put_main(e, stk, start, values):
         put(stk, start + 1, values, 0.0, 0.0)
         rows = pl.ds(start_of(start // CHUNK) if isinstance(start, int) else pl.multiple_of(start, CHUNK), CHUNK)
-        out_col[e, 0, rows] = values[:, 0, :]
-        out_col[e, 1, rows] = values[:, width - 1, :]
+        for side in range(2):
+            @pl.when(exists(0, 2 * side - 1))
+            def _(side=side):
+                part = pl.ds(0, 16) if side == 0 else pl.ds(width - 16, 16)
+                near = stk[pl.ds(start + 1, CHUNK), part, chan : 2 * chan].astype(jnp.float32)
+                out_col[e, side, rows] = near[:, 15 * side, :]
 
     def fix_row(e, stk, side):
         for d, (dr, dc) in enumerate(DIRECTIONS):

time: 38.6 us -> 38.6 us (level)
  no operation moved by 1% of the time
where the time goes in v6:
time: 38.6 us; the launch traced here: 37.9 us
  Pallas kernels  35.7 us (92%)
  local copies, waits for them, and re-layouts  2.26 us (6%)
    pallas_call x1, Pallas kernels, per_device(): pl.pallas_call(functools.partial(kernel, *sizes), out_shape=jax.ShapeDtyp...  35.7 us
    unnamed x1, local copies, waits for them, and re-layouts  2.26 us

profile of v6, /device:TPU:17, one launch (start us, length us, event | category | flops | bytes accessed | tf_op | source)
XLA Modules:
  0.0 37.9 jit_solution(10778304897928400300)
XLA Ops:
  0.0 35.7 %shard_map.64 = bf16[2,32,32,256]{3,2,1,0:T(8,128)(2,1)} custom-call(bf16[32,32,256]{2,1,0:T(8,128)(2,1)} %bitcast.11, bf16[32,32,256]{2,1,0:T(8,128)(2,1)} %fresh.1, bf16[3,768,256]{2,1,0:T(8,128)(2,1)} %bitcast.9, bf16[3,768,256]{2,1,0:T(8,128)(2,1)} %bitcast.10, f32[2,256]{1,0:T(2,128)} %bitcast.12, f32[2,256]{1,0:T(2,128)} %bitcast.13), custom_call_target="tpu_custom_call" | custom-call | tf_op jit(solution)/shard_map/pallas_call | solution.py:332
  35.7 2.3 %copy.9 = bf16[2,1,32,32,256]{4,3,2,1,0:T(8,128)(2,1)} copy(bf16[2,1,32,32,256]{4,3,2,1,0:T(8,128)(2,1)} %bitcast.8) | data formatting | bytes 2097152
